TPU v7x, 512 devices: a whole 4x8x8 slice. The times are simulated.
512 devices in a mesh: cp: 128 (over y, z, core), hp: 4 (over x).
Axes of the slice: x: 4, y: 8, z: 8, core: 2. Of those that a mesh axis runs over, the one named last changes fastest.
Arguments:
- queries: bfloat16 [32768, 3072], P('cp', 'hp'), may hold values from -40 to 40
- key_rows: bfloat16 [32768, 3072], P('cp', 'hp'), may hold values from -4 to 4
- value_rows: bfloat16 [32768, 3072], P('cp', 'hp'), may hold values from -6 to 6
- out_grad: bfloat16 [32768, 3072], P('cp', 'hp'), may hold values from -6 to 6
- slot_stretch: int32 [256], replicated, may hold values from 0 to 255, as said below
- doc_id: int32 [256], replicated, may hold values from 0 to 255, as said below
- diag_kind: int32 [256], replicated, may hold values 0 or 1
Outputs:
- attended: bfloat16 [32768, 3072], P(('cp', 'hp'))
- query_grad: bfloat16 [32768, 3072], P(('cp', 'hp'))
- key_grad: bfloat16 [32768, 3072], P(('cp', 'hp'))
- value_grad: bfloat16 [32768, 3072], P(('cp', 'hp'))
Inputs may be any that keep to these rules, and one draw needn't show every extreme that they name: `slot_stretch`: each stretch number once; the slots w * 16 to w * 16 + 15 hold the stretches w * 16 to w * 16 + 15 in some order. `doc_id`: a document's id is the number of its first stretch; it never falls from one stretch to the next and changes at every stretch w * 16, so no document spans two windows.
All inputs are finite; a program needn't handle non-finite values.
Results may differ from a plain program's by a relative error of at most 0.015.
The roundings to bfloat16 on the way count: a program that leaves them out, or rounds other values in their place, can miss the bound.
Values may be sent and summed in bfloat16 or wider, within the bound.
A program may use at most 64 MiB of HBM per device.

v0:
```python
import math

import jax
import jax.numpy as jnp
from jax import lax
from jax.sharding import PartitionSpec as P

HEAD_DIM = 128
CH_DEV = 2
WIN_MOST = 16


def swapped(array, axis, apart):
    return lax.ppermute(array, axis, [(i, i ^ 1 << apart) for i in range(lax.axis_size(axis))])


def lookup(lookup_table, positions):
    matches = positions[:, None] == jnp.arange(lookup_table.shape[0])[None, :]
    return jnp.sum(jnp.where(matches, lookup_table[None, :], 0), axis=1)


def pair_mask(query_stretches, query_docs, query_kinds, key_stretches, key_docs, block_len):
    same_doc = query_docs[:, None] == key_docs[None, :]
    earlier = key_stretches[None, :] < query_stretches[:, None]
    same_stretch = key_stretches[None, :] == query_stretches[:, None]
    row_index = jnp.arange(block_len)
    lower_tri = row_index[None, :] <= row_index[:, None]
    full_diag = (query_kinds == 0)[:, None, None, None]
    inside = same_stretch[:, None, :, None] & (full_diag | lower_tri[None, :, None, :])
    return same_doc[:, None, :, None] & (earlier[:, None, :, None] | inside)


def join_pair(holding, arrived, upper_bit, axis_dim):
    return jnp.where(
        upper_bit == 1,
        jnp.concatenate([arrived, holding], axis_dim),
        jnp.concatenate([holding, arrived], axis_dim),
    )


def heads_to_rows(stacked):
    return jnp.transpose(stacked, (1, 0, 2)).reshape(
        stacked.shape[1], stacked.shape[0] * stacked.shape[2]
    )


def query_side(head_index, own_queries, own_grads, keys_all, values_all, allowed, stretch_count):
    first_col = head_index * HEAD_DIM
    head_queries = lax.dynamic_slice_in_dim(own_queries, first_col, HEAD_DIM, 1)
    head_grads = lax.dynamic_slice_in_dim(own_grads, first_col, HEAD_DIM, 1)
    head_keys = lax.dynamic_slice_in_dim(keys_all, first_col, HEAD_DIM, 1)
    head_values = lax.dynamic_slice_in_dim(values_all, first_col, HEAD_DIM, 1)
    score_scale = 1.0 / math.sqrt(HEAD_DIM)
    scores = (
        jnp.einsum("qd,kd->qk", head_queries, head_keys, preferred_element_type=jnp.float32)
        * score_scale
    )
    masked = jnp.where(allowed, scores, -1e30)
    row_max = jnp.max(masked, axis=1, keepdims=True)
    exponent = jnp.where(allowed, jnp.exp(masked - row_max), 0.0)
    row_total = jnp.sum(exponent, axis=1, keepdims=True)
    weights = exponent / row_total
    rounded = weights.astype(jnp.bfloat16)
    attended = lax.optimization_barrier(
        jnp.dot(rounded, head_values, preferred_element_type=jnp.float32).astype(jnp.bfloat16)
    )
    grad_dot = jnp.sum(
        head_grads.astype(jnp.float32) * attended.astype(jnp.float32), axis=1, keepdims=True
    )
    weight_grad = jnp.einsum(
        "qd,kd->qk", head_grads, head_values, preferred_element_type=jnp.float32
    )
    score_grad = (weights * (weight_grad - grad_dot)).astype(jnp.bfloat16)
    query_grad = (
        jnp.dot(score_grad, head_keys, preferred_element_type=jnp.float32) * score_scale
    ).astype(jnp.bfloat16)
    row_count = head_queries.shape[0] // stretch_count
    key_term = (
        jnp.einsum(
            "cqk,cqd->ckd",
            score_grad.reshape(stretch_count, row_count, -1),
            head_queries.reshape(stretch_count, row_count, HEAD_DIM),
            preferred_element_type=jnp.float32,
        )
        * score_scale
    )
    key_part = jnp.sum(
        lax.optimization_barrier(key_term.astype(jnp.bfloat16)).astype(jnp.float32), axis=0
    ).astype(jnp.bfloat16)
    value_term = jnp.einsum(
        "cqk,cqd->ckd",
        rounded.reshape(stretch_count, row_count, -1),
        head_grads.reshape(stretch_count, row_count, HEAD_DIM),
        preferred_element_type=jnp.float32,
    )
    value_part = jnp.sum(
        lax.optimization_barrier(value_term.astype(jnp.bfloat16)).astype(jnp.float32), axis=0
    ).astype(jnp.bfloat16)
    return (attended, query_grad, key_part, value_part)


def body(queries, key_rows, value_rows, out_grad, slot_stretch, doc_id, diag_kind):
    own_queries, own_keys, own_values, own_grads = (queries, key_rows, value_rows, out_grad)
    heads_here = own_queries.shape[1] // HEAD_DIM
    stretch_count = CH_DEV
    block_len = own_queries.shape[0] // stretch_count
    groups = min(WIN_MOST // CH_DEV, lax.axis_size("cp") // 2)
    sections = groups.bit_length() - 1
    window_len = groups * stretch_count
    position = lax.axis_index("cp")
    in_group = position % groups
    window_start = (position - in_group) * stretch_count
    window_stretches = lax.dynamic_slice_in_dim(slot_stretch, window_start, window_len)
    window_docs = lax.dynamic_slice_in_dim(doc_id, window_start, window_len)
    window_kinds = lax.dynamic_slice_in_dim(diag_kind, window_start, window_len)
    stretch_docs = lookup(window_docs, window_stretches - window_start)
    stretch_kinds = lookup(window_kinds, window_stretches - window_start)
    my_stretches = lax.dynamic_slice_in_dim(
        window_stretches, in_group * stretch_count, stretch_count
    )
    my_docs = lax.dynamic_slice_in_dim(stretch_docs, in_group * stretch_count, stretch_count)
    my_kinds = lax.dynamic_slice_in_dim(stretch_kinds, in_group * stretch_count, stretch_count)
    allowed = pair_mask(
        my_stretches, my_docs, my_kinds, window_stretches, stretch_docs, block_len
    ).reshape(stretch_count * block_len, window_len * block_len)
    keys_all, values_all = (own_keys, own_values)
    for section_bit in range(sections):
        upper_bit = in_group // 2**section_bit % 2
        arrived_keys, arrived_values = swapped((keys_all, values_all), "cp", section_bit)
        keys_all = join_pair(keys_all, arrived_keys, upper_bit, 0)
        values_all = join_pair(values_all, arrived_values, upper_bit, 0)
    head_list = jnp.arange(heads_here)

    def per_head(head_index):
        return query_side(
            head_index, own_queries, own_grads, keys_all, values_all, allowed, stretch_count
        )

    attended, query_grad, key_sums, value_sums = lax.map(per_head, head_list)
    for section_bit in reversed(range(sections)):
        upper_bit = in_group // 2**section_bit % 2
        half_rows = key_sums.shape[1] // 2
        kept_keys = jnp.where(upper_bit == 1, key_sums[:, half_rows:], key_sums[:, :half_rows])
        sent_keys = jnp.where(upper_bit == 1, key_sums[:, :half_rows], key_sums[:, half_rows:])
        kept_values = jnp.where(
            upper_bit == 1, value_sums[:, half_rows:], value_sums[:, :half_rows]
        )
        sent_values = jnp.where(
            upper_bit == 1, value_sums[:, :half_rows], value_sums[:, half_rows:]
        )
        arrived_keys, arrived_values = swapped((sent_keys, sent_values), "cp", section_bit)
        key_sums = lax.optimization_barrier(
            (kept_keys.astype(jnp.float32) + arrived_keys.astype(jnp.float32)).astype(jnp.bfloat16)
        )
        value_sums = lax.optimization_barrier(
            (kept_values.astype(jnp.float32) + arrived_values.astype(jnp.float32)).astype(
                jnp.bfloat16
            )
        )
    key_grad, value_grad = (key_sums, value_sums)
    attended_out = lax.all_to_all(
        heads_to_rows(attended), "hp", split_axis=0, concat_axis=1, tiled=True
    )
    query_out, key_out, value_out = (
        lax.all_to_all(heads_to_rows(query_grad), "hp", split_axis=0, concat_axis=1, tiled=True),
        lax.all_to_all(heads_to_rows(key_grad), "hp", split_axis=0, concat_axis=1, tiled=True),
        lax.all_to_all(heads_to_rows(value_grad), "hp", split_axis=0, concat_axis=1, tiled=True),
    )
    return (attended_out, query_out, key_out, value_out)


def solution(mesh):
    in_specs = (P("cp", "hp"), P("cp", "hp"), P("cp", "hp"), P("cp", "hp"), P(), P(), P())
    out_specs = (
        P(("cp", "hp"), None),
        P(("cp", "hp"), None),
        P(("cp", "hp"), None),
        P(("cp", "hp"), None),
    )
    return jax.shard_map(body, mesh=mesh, in_specs=in_specs, out_specs=out_specs, check_vma=False)
```

profile of v0, /device:TPU:1, one launch (start us, length us, event | category | flops | bytes accessed | tf_op | source)
XLA Modules:
  0.0 485.2 jit_solution(920883314299907974)
XLA Ops:
  0.6 8.8 %collective-permute-start = (bf16[256,768]{1,0:T(8,128)(2,1)}, bf16[256,768]{1,0:T(8,128)(2,1)S(1)}, u32[]{:S(2)}, u32[]{:S(2)}) collective-permute-start(bf16[256,768]{1,0:T(8,128)(2,1)} %param.10), channel_id=1, source_target_pairs={{0,4},{4,0},{8,12},{12,8},{16,20},{20,16},{24,28},{28,24},{32,36},... | collective-permute-start | bytes 1179656 | tf_op jit(solution)/shard_map/ppermute | solution.py:14
  9.4 1.9 collective-permute-start.3
  12.7 1.9 collective-permute-start.1
  16.0 3.4 collective-permute-start.4
  19.5 13.9 %collective-permute-done.1 = bf16[512,768]{1,0:T(8,128)(2,1)} collective-permute-done((bf16[512,768]{1,0:T(8,128)(2,1)S(1)}, bf16[512,768]{1,0:T(8,128)(2,1)}, u32[]{:S(2)}, u32[]{:S(2)}) %collective-permute-start.1) | collective-permute-done | bytes 786464 | tf_op jit(solution)/shard_map/ppermute | solution.py:14
  33.4 1.9 maximum_select_fusion.2
  35.3 2.1 collective-permute-start.2
  37.4 21.9 %collective-permute-done.4 = bf16[512,768]{1,0:T(8,128)(2,1)} collective-permute-done((bf16[512,768]{1,0:T(8,128)(2,1)S(1)}, bf16[512,768]{1,0:T(8,128)(2,1)}, u32[]{:S(2)}, u32[]{:S(2)}) %collective-permute-start.4) | collective-permute-done | bytes 786464 | tf_op jit(solution)/shard_map/ppermute | solution.py:14
  59.2 2.3 maximum_select_fusion.3
  61.6 2.8 collective-permute-start.5
  65.4 74.0 %collective-permute-done.2 = bf16[1024,768]{1,0:T(8,128)(2,1)} collective-permute-done((bf16[1024,768]{1,0:T(8,128)(2,1)S(1)}, bf16[1024,768]{1,0:T(8,128)(2,1)}, u32[]{:S(2)}, u32[]{:S(2)}) %collective-permute-start.2) | collective-permute-done | bytes 1572896 | tf_op jit(solution)/shard_map/ppermute | solution.py:14
  139.4 3.5 maximum_select_fusion
  142.9 30.2 %collective-permute-done.5 = bf16[1024,768]{1,0:T(8,128)(2,1)} collective-permute-done((bf16[1024,768]{1,0:T(8,128)(2,1)S(1)}, bf16[1024,768]{1,0:T(8,128)(2,1)}, u32[]{:S(2)}, u32[]{:S(2)}) %collective-permute-start.5) | collective-permute-done | bytes 1572896 | tf_op jit(solution)/shard_map/ppermute | solution.py:14
  173.1 3.5 maximum_select_fusion.1
  176.7 95.5 %while.20 = (s32[]{:T(128)}, bf16[6,256,128]{2,1,0:T(8,128)(2,1)}, bf16[6,256,128]{2,1,0:T(8,128)(2,1)}, bf16[6,2048,128]{2,1,0:T(8,128)(2,1)}, bf16[6,2048,128]...) while((s32[]{:T(128)}, bf16[6,256,128]{2,1,0:T(8,128)(2,1)}, ...), condition=%wide.region_8.9_spmd.clone, body=%wide.region_2.8_spmd.clone.sunk | while | flops 817593600 | bytes 27634036 | solution.py:139
  184.8 1.9 fusion.57
  188.4 2.1 fusion.58
  200.7 1.9 fusion.57
  204.3 2.1 fusion.58
  211.1 1.8 fusion.54
  216.6 1.9 fusion.57
  220.2 2.1 fusion.58
  232.5 1.9 fusion.57
  236.1 2.1 fusion.58
  242.9 1.8 fusion.54
  248.5 1.9 fusion.57
  252.0 2.1 fusion.58
  264.4 1.9 fusion.57
  268.0 2.1 fusion.58
  272.2 2.2 broadcast_select_fusion.1
  274.4 1.9 collective-permute-start.6
  276.5 4.4 collective-permute-start.9
  280.9 98.0 %collective-permute-done.6 = bf16[6,1024,128]{2,1,0:T(8,128)(2,1)S(1)} collective-permute-done((bf16[6,1024,128]{2,1,0:T(8,128)(2,1)S(1)}, bf16[6,1024,128]{2,1,0:T(8,128)(2,1)S(1)}, u32[]{:S(2)}, u32[]{:S(2)}) %collective-permute-start.6) | collective-permute-done | bytes 1572896 | tf_op jit(solution)/shard_map/ppermute | solution.py:14
  380.5 1.9 collective-permute-start.7
  382.4 30.2 %collective-permute-done.9 = bf16[6,1024,128]{2,1,0:T(8,128)(2,1)S(1)} collective-permute-done((bf16[6,1024,128]{2,1,0:T(8,128)(2,1)S(1)}, bf16[6,1024,128]{2,1,0:T(8,128)(2,1)S(1)}, u32[]{:S(2)}, u32[]{:S(2)}) %collective-permute-start.9) | collective-permute-done | bytes 1572896 | tf_op jit(solution)/shard_map/ppermute | solution.py:14
  414.3 2.1 collective-permute-start.10
  417.5 2.2 all_to_all.60
  419.7 4.0 all-to-all-start.1
  423.7 5.8 %collective-permute-done.7 = bf16[6,512,128]{2,1,0:T(8,128)(2,1)} collective-permute-done((bf16[6,512,128]{2,1,0:T(8,128)(2,1)}, bf16[6,512,128]{2,1,0:T(8,128)(2,1)}, u32[]{:S(2)}, u32[]{:S(2)}) %collective-permute-start.7) | collective-permute-done | bytes 786464 | tf_op jit(solution)/shard_map/ppermute | solution.py:14
  431.9 2.6 collective-permute-start.8
  434.5 11.9 %collective-permute-done.10 = bf16[6,512,128]{2,1,0:T(8,128)(2,1)} collective-permute-done((bf16[6,512,128]{2,1,0:T(8,128)(2,1)}, bf16[6,512,128]{2,1,0:T(8,128)(2,1)}, u32[]{:S(2)}, u32[]{:S(2)}) %collective-permute-start.10) | collective-permute-done | bytes 786464 | tf_op jit(solution)/shard_map/ppermute | solution.py:14
  448.7 2.5 collective-permute-start.11
  452.7 4.0 all-to-all-start
  459.4 5.3 %all-to-all-done = bf16[4,64,768]{2,1,0:T(8,128)(2,1)S(1)} async-done(((bf16[4,64,768]{2,1,0:T(8,128)(2,1)}), bf16[4,64,768]{2,1,0:T(8,128)(2,1)S(1)}, u32[]{:S(2)}, u32[]{:S(2)}) %all-to-all-start) | async-done | bytes 393248 | tf_op jit(solution)/shard_map/all_to_all | solution.py:161
  464.7 3.5 all-to-all-start.2
  469.8 5.0 %all-to-all-done.2 = bf16[4,64,768]{2,1,0:T(8,128)(2,1)S(1)} async-done(((bf16[4,64,768]{2,1,0:T(8,128)(2,1)}), bf16[4,64,768]{2,1,0:T(8,128)(2,1)S(1)}, u32[]{:S(2)}, u32[]{:S(2)}) %all-to-all-start.2) | async-done | bytes 393248 | tf_op jit(solution)/shard_map/all_to_all | solution.py:166
  474.8 3.5 all-to-all-start.3
  480.6 3.9 all-to-all-done.3
  (147 shorter events, 85.5 us)
Async XLA Ops:
  0.6 10.8 %collective-permute-start = (bf16[256,768]{1,0:T(8,128)(2,1)}, bf16[256,768]{1,0:T(8,128)(2,1)S(1)}, u32[]{:S(2)}, u32[]{:S(2)}) collective-permute-start(bf16[256,768]{1,0:T(8,128)(2,1)} %param.10), channel_id=1, source_target_pairs={{0,4},{4,0},{8,12},{12,8},{16,20},{20,16},{24,28},{28,24},{32,36},... | collective-permute-start | bytes 1179656 | tf_op jit(solution)/shard_map/ppermute | solution.py:14
  9.4 5.3 %collective-permute-start.3 = (bf16[256,768]{1,0:T(8,128)(2,1)}, bf16[256,768]{1,0:T(8,128)(2,1)S(1)}, u32[]{:S(2)}, u32[]{:S(2)}) collective-permute-start(bf16[256,768]{1,0:T(8,128)(2,1)} %param.11), channel_id=1, source_target_pairs={{0,4},{4,0},{8,12},{12,8},{16,20},{20,16},{24,28},{28,24},{32,36},... | collective-permute-start | bytes 1179656 | tf_op jit(solution)/shard_map/ppermute | solution.py:14
  12.7 20.6 %collective-permute-start.1 = (bf16[512,768]{1,0:T(8,128)(2,1)S(1)}, bf16[512,768]{1,0:T(8,128)(2,1)}, u32[]{:S(2)}, u32[]{:S(2)}) collective-permute-start(bf16[512,768]{1,0:T(8,128)(2,1)S(1)} %maximum_select_fusion.4), channel_id=1, source_target_pairs={{0,8},{4,12},{8,0},{12,4},{16,24},{20,28},{24,16},{28,20},{32,40},... | collective-permute-start | bytes 2359304 | tf_op jit(solution)/shard_map/ppermute | solution.py:14
  16.0 21.3 %copy-start.4 = (bf16[512,768]{1,0:T(8,128)(2,1)}, bf16[512,768]{1,0:T(8,128)(2,1)S(1)}, u32[]{:S(2)}) copy-start(bf16[512,768]{1,0:T(8,128)(2,1)S(1)} %maximum_select_fusion.5) | copy-start | bytes 2359300
  16.0 43.2 %collective-permute-start.4 = (bf16[512,768]{1,0:T(8,128)(2,1)S(1)}, bf16[512,768]{1,0:T(8,128)(2,1)}, u32[]{:S(2)}, u32[]{:S(2)}) collective-permute-start(bf16[512,768]{1,0:T(8,128)(2,1)S(1)} %maximum_select_fusion.5), channel_id=1, source_target_pairs={{0,8},{4,12},{8,0},{12,4},{16,24},{20,28},{24,16},{28,20},{32,40},... | collective-permute-start | bytes 2359304 | tf_op jit(solution)/shard_map/ppermute | solution.py:14
  35.3 29.2 %copy-start.8 = (s32[256]{0:T(256)S(1)}, s32[256]{0:T(256)}, u32[]{:S(2)}) copy-start(s32[256]{0:T(256)} %param.14) | copy-start | bytes 3076
  35.3 29.3 %copy-start.9 = (s32[256]{0:T(256)S(1)}, s32[256]{0:T(256)}, u32[]{:S(2)}) copy-start(s32[256]{0:T(256)} %param.15) | copy-start | bytes 3076
  35.3 29.4 %copy-start.7 = (s32[256]{0:T(256)S(1)}, s32[256]{0:T(256)}, u32[]{:S(2)}) copy-start(s32[256]{0:T(256)} %param.13) | copy-start | bytes 3076
  35.3 104.1 %collective-permute-start.2 = (bf16[1024,768]{1,0:T(8,128)(2,1)S(1)}, bf16[1024,768]{1,0:T(8,128)(2,1)}, u32[]{:S(2)}, u32[]{:S(2)}) collective-permute-start(bf16[1024,768]{1,0:T(8,128)(2,1)S(1)} %maximum_select_fusion.2), channel_id=1, source_target_pairs={{0,16},{4,20},{8,24},{12,28},{16,0},{20,4},{24,8},{28,12},{32,48},... | collective-permute-start | bytes 4718600 | tf_op jit(solution)/shard_map/ppermute | solution.py:14
  61.6 111.6 %collective-permute-start.5 = (bf16[1024,768]{1,0:T(8,128)(2,1)S(1)}, bf16[1024,768]{1,0:T(8,128)(2,1)}, u32[]{:S(2)}, u32[]{:S(2)}) collective-permute-start(bf16[1024,768]{1,0:T(8,128)(2,1)S(1)} %maximum_select_fusion.3), channel_id=1, source_target_pairs={{0,16},{4,20},{8,24},{12,28},{16,0},{20,4},{24,8},{28,12},{32,48},... | collective-permute-start | bytes 4718600 | tf_op jit(solution)/shard_map/ppermute | solution.py:14
  272.2 4.1 copy-start
  274.4 104.5 %collective-permute-start.6 = (bf16[6,1024,128]{2,1,0:T(8,128)(2,1)S(1)}, bf16[6,1024,128]{2,1,0:T(8,128)(2,1)S(1)}, u32[]{:S(2)}, u32[]{:S(2)}) collective-permute-start(bf16[6,1024,128]{2,1,0:T(8,128)(2,1)S(1)} %broadcast_select_fusion.1), channel_id=1, source_target_pairs={{0,16},{4,20},{8,24},{12,28},{16,0},{20,4},{24,8},{28,12},{32,48},... | collective-permute-start | bytes 4718600 | tf_op jit(solution)/shard_map/ppermute | solution.py:14
  276.3 102.6 %copy-start.1 = (bf16[6,2048,128]{2,1,0:T(8,128)(2,1)S(1)}, bf16[6,2048,128]{2,1,0:T(8,128)(2,1)}, u32[]{:S(2)}) copy-start(bf16[6,2048,128]{2,1,0:T(8,128)(2,1)} %get-tuple-element.174) | copy-start | bytes 9437188
  276.5 136.1 %collective-permute-start.9 = (bf16[6,1024,128]{2,1,0:T(8,128)(2,1)S(1)}, bf16[6,1024,128]{2,1,0:T(8,128)(2,1)S(1)}, u32[]{:S(2)}, u32[]{:S(2)}) collective-permute-start(bf16[6,1024,128]{2,1,0:T(8,128)(2,1)S(1)} %broadcast_select_fusion), channel_id=1, source_target_pairs={{0,16},{4,20},{8,24},{12,28},{16,0},{20,4},{24,8},{28,12},{32,48},... | collective-permute-start | bytes 4718600 | tf_op jit(solution)/shard_map/ppermute | solution.py:14
  380.5 49.1 %collective-permute-start.7 = (bf16[6,512,128]{2,1,0:T(8,128)(2,1)}, bf16[6,512,128]{2,1,0:T(8,128)(2,1)}, u32[]{:S(2)}, u32[]{:S(2)}) collective-permute-start(bf16[6,512,128]{2,1,0:T(8,128)(2,1)} %broadcast_select_fusion.3), channel_id=1, source_target_pairs={{0,8},{4,12},{8,0},{12,4},{16,24},{20,28},{24,16},{28,20},{32,40},... | collective-permute-start | bytes 2359304 | tf_op jit(solution)/shard_map/ppermute | solution.py:14
  413.3 3.1 copy-start.5
  414.3 32.2 %collective-permute-start.10 = (bf16[6,512,128]{2,1,0:T(8,128)(2,1)}, bf16[6,512,128]{2,1,0:T(8,128)(2,1)}, u32[]{:S(2)}, u32[]{:S(2)}) collective-permute-start(bf16[6,512,128]{2,1,0:T(8,128)(2,1)} %broadcast_select_fusion.2), channel_id=1, source_target_pairs={{0,8},{4,12},{8,0},{12,4},{16,24},{20,28},{24,16},{28,20},{32,40},... | collective-permute-start | bytes 2359304 | tf_op jit(solution)/shard_map/ppermute | solution.py:14
  419.7 33.0 %all-to-all-start.1 = ((bf16[4,64,768]{2,1,0:T(8,128)(2,1)}), bf16[4,64,768]{2,1,0:T(8,128)(2,1)S(1)}, u32[]{:S(2)}, u32[]{:S(2)}) async-start(bf16[4,64,768]{2,1,0:T(8,128)(2,1)} %all_to_all.60), calls=%async_computation.1 | async-start | bytes 786432 | tf_op jit(solution)/shard_map/all_to_all | solution.py:165
  431.0 16.9 %copy-start.2 = (bf16[6,512,128]{2,1,0:T(8,128)(2,1)}, bf16[6,512,128]{2,1,0:T(8,128)(2,1)S(1)}, u32[]{:S(2)}) copy-start(bf16[6,512,128]{2,1,0:T(8,128)(2,1)S(1)} %add_convert_fusion.3) | copy-start | bytes 2359300
  431.9 19.3 %copy-start.6 = (bf16[6,256,128]{2,1,0:T(8,128)(2,1)S(1)}, bf16[6,256,128]{2,1,0:T(8,128)(2,1)}, u32[]{:S(2)}) copy-start(bf16[6,256,128]{2,1,0:T(8,128)(2,1)} %get-tuple-element.172) | copy-start | bytes 1179652
  431.9 24.8 %collective-permute-start.8 = (bf16[6,256,128]{2,1,0:T(8,128)(2,1)}, bf16[6,256,128]{2,1,0:T(8,128)(2,1)}, u32[]{:S(2)}, u32[]{:S(2)}) collective-permute-start(bf16[6,256,128]{2,1,0:T(8,128)(2,1)} %broadcast_select_fusion.5), channel_id=1, source_target_pairs={{0,4},{4,0},{8,12},{12,8},{16,20},{20,16},{24,28},{28,24},{32,36},... | collective-permute-start | bytes 1179656 | tf_op jit(solution)/shard_map/ppermute | solution.py:14
  448.7 8.1 %copy-start.3 = (bf16[6,512,128]{2,1,0:T(8,128)(2,1)S(1)}, bf16[6,512,128]{2,1,0:T(8,128)(2,1)}, u32[]{:S(2)}) copy-start(bf16[6,512,128]{2,1,0:T(8,128)(2,1)} %copy-done.2) | copy-start | bytes 2359300
  448.7 19.4 %collective-permute-start.11 = (bf16[6,256,128]{2,1,0:T(8,128)(2,1)}, bf16[6,256,128]{2,1,0:T(8,128)(2,1)S(1)}, u32[]{:S(2)}, u32[]{:S(2)}) collective-permute-start(bf16[6,256,128]{2,1,0:T(8,128)(2,1)} %broadcast_select_fusion.4), channel_id=1, source_target_pairs={{0,4},{4,0},{8,12},{12,8},{16,20},{20,16},{24,28},{28,24},{32,36},... | collective-permute-start | bytes 1179656 | tf_op jit(solution)/shard_map/ppermute | solution.py:14
  452.7 11.9 %all-to-all-start = ((bf16[4,64,768]{2,1,0:T(8,128)(2,1)}), bf16[4,64,768]{2,1,0:T(8,128)(2,1)S(1)}, u32[]{:S(2)}, u32[]{:S(2)}) async-start(bf16[4,64,768]{2,1,0:T(8,128)(2,1)} %all_to_all.56), calls=%async_computation | async-start | bytes 786432 | tf_op jit(solution)/shard_map/all_to_all | solution.py:161
  464.7 10.1 %all-to-all-start.2 = ((bf16[4,64,768]{2,1,0:T(8,128)(2,1)}), bf16[4,64,768]{2,1,0:T(8,128)(2,1)S(1)}, u32[]{:S(2)}, u32[]{:S(2)}) async-start(bf16[4,64,768]{2,1,0:T(8,128)(2,1)} %all_to_all.64), calls=%async_computation.2 | async-start | bytes 786432 | tf_op jit(solution)/shard_map/all_to_all | solution.py:166
  474.8 9.7 %all-to-all-start.3 = ((bf16[4,64,768]{2,1,0:T(8,128)(2,1)}), bf16[4,64,768]{2,1,0:T(8,128)(2,1)S(1)}, u32[]{:S(2)}, u32[]{:S(2)}) async-start(bf16[4,64,768]{2,1,0:T(8,128)(2,1)} %all_to_all.68), calls=%async_computation.3 | async-start | bytes 786432 | tf_op jit(solution)/shard_map/all_to_all | solution.py:167
where the time goes:
time: 490 us; the launch traced here: 485 us
  waiting for transfers between devices  300 us (61%)
  starting transfers between devices  51.3 us (10%)
  matrix products  49.7 us (10%)
  other arithmetic  48.7 us (10%)
  local copies, waits for them, and re-layouts  30 us (6%)
    ppermute x12, waiting for transfers between devices, swapped(): lax.ppermute(array, axis, [(i, i ^ 1 << apart) for i in range(lax.axis_si...  286 us
    ppermute x12, starting transfers between devices, swapped(): lax.ppermute(array, axis, [(i, i ^ 1 << apart) for i in range(lax.axis_si...  36.3 us
    select_n x6, other arithmetic, join_pair(): jnp.where(upper_bit == 1, jnp.concatenate([arrived, holding], axis_dim),...  13.9 us
    dot_general x6, matrix products, query_side(): jnp.dot(score_grad, head_keys, preferred_element_type=jnp.float32)  12.6 us
    dot_general x6, matrix products, query_side(): jnp.einsum('qd,kd->qk', head_grads, head_values, preferred_element_type=j...  11.2 us
    dot_general x6, matrix products, query_side(): jnp.einsum('qd,kd->qk', head_queries, head_keys, preferred_element_type=j...  10.6 us
    dynamic_update_slice x12, local copies, waits for them, and re-layouts, body(): attended, query_grad, key_sums, value_sums = lax.map(per_head, head_list)  10.2 us
  transfers between devices with their start and end apart: 16, of which 11 were waited for; matrix products, arithmetic and copies ran while one was open for 5% of the time, Pallas kernels for 0%

commit v1 on v0

v1 whole, which is shorter than its diff:
```python
import functools
import math

import jax
import jax.numpy as jnp
from jax import lax
from jax.experimental import pallas as pl
from jax.experimental.pallas import tpu as pltpu
from jax.sharding import PartitionSpec as P

HEAD_DIM = 128
BLOCK = 128
WIN = 16
GROUP = 8
HEADS_HERE = 6
HP = 4
PIECE = 64
PIECES = WIN * BLOCK // PIECE
ARRAYS = 4
MESH = pl.DeviceIdType.MESH
SCALE = 1.0 / math.sqrt(HEAD_DIM)
CHUNK = 256


def owner_of(head):
    return head + jnp.where(head >= 1, 1, 0) + jnp.where(head >= 5, 1, 0)


def head_of(member):
    return member - jnp.where(member >= 2, 1, 0) - jnp.where(member >= 7, 1, 0)


def is_owner(member):
    return (member != 1) & (member != 6)


def spread_kernel(*refs):
    sources, (landed, send_sem, recv_sem) = refs[:ARRAYS], refs[ARRAYS:]
    cp, hp = lax.axis_index("cp"), lax.axis_index("hp")
    member = lax.rem(cp, GROUP)
    first = cp - member
    owner = is_owner(member)

    barrier = pltpu.get_barrier_semaphore()

    @pl.when(owner)
    def _():
        for other in range(1, GROUP):
            peer = first + lax.rem(member + other, GROUP)
            pl.semaphore_signal(barrier, inc=1, device_id=(peer, hp), device_id_type=MESH)

    pl.semaphore_wait(barrier, HEADS_HERE - jnp.where(owner, 1, 0))

    rows = pl.ds(pl.multiple_of(member * 2 * BLOCK, 2 * BLOCK), 2 * BLOCK)

    def remote(array, step):
        head = jnp.where(member < GROUP // 2, HEADS_HERE - 1 - step, step)
        target = owner_of(head)
        columns = pl.ds(pl.multiple_of(head * HEAD_DIM, HEAD_DIM), HEAD_DIM)
        return target, pltpu.make_async_remote_copy(
            src_ref=sources[array].at[:, columns],
            dst_ref=landed.at[array, rows],
            send_sem=send_sem.at[array, step],
            recv_sem=recv_sem.at[array, member],
            device_id=(first + target, hp),
            device_id_type=MESH,
        )

    def local(array):
        columns = pl.ds(pl.multiple_of(head_of(member) * HEAD_DIM, HEAD_DIM), HEAD_DIM)
        return pltpu.make_async_copy(
            sources[array].at[:, columns], landed.at[array, rows], recv_sem.at[array, member]
        )

    for array in range(ARRAYS):
        for step in range(HEADS_HERE):
            target, copy = remote(array, step)

            @pl.when(target != member)
            def _(copy=copy):
                copy.start()

        @pl.when(owner)
        def _(array=array):
            local(array).start()

    for array in range(ARRAYS):
        for step in range(HEADS_HERE):
            target, copy = remote(array, step)

            @pl.when(target != member)
            def _(copy=copy):
                copy.wait_send()

    @pl.when(owner)
    def _():
        for array in range(ARRAYS):
            for source in range(GROUP):
                pltpu.make_async_copy(
                    landed.at[array, pl.ds(source * 2 * BLOCK, 2 * BLOCK)],
                    landed.at[array, pl.ds(source * 2 * BLOCK, 2 * BLOCK)],
                    recv_sem.at[array, source],
                ).wait()


def spread(arrays):
    return pl.pallas_call(
        spread_kernel,
        name="spread_heads",
        out_shape=jax.ShapeDtypeStruct((ARRAYS, WIN * BLOCK, HEAD_DIM), jnp.bfloat16),
        in_specs=[pl.BlockSpec(memory_space=pl.ANY)] * ARRAYS,
        out_specs=pl.BlockSpec(memory_space=pl.ANY),
        scratch_shapes=[
            pltpu.SemaphoreType.DMA((ARRAYS, HEADS_HERE)),
            pltpu.SemaphoreType.DMA((ARRAYS, GROUP)),
        ],
        compiler_params=pltpu.CompilerParams(collective_id=0, has_side_effects=True),
    )(*arrays)


def matmul(left, right, left_dim, right_dim):
    return lax.dot_general(
        left, right, (((left_dim,), (right_dim,)), ((), ())), preferred_element_type=jnp.float32
    )


def attend_tile(width, stretch, slot, low, kind, refs):
    given, out, keys, values, key_acc, value_acc, scores, grads = refs
    chunks = width // CHUNK
    query, out_grad = given[0, slot], given[3, slot]
    base = jnp.maximum(stretch + 1 - width // BLOCK, 0)
    row = lax.broadcasted_iota(jnp.int32, (BLOCK, 1), 0)
    top = jnp.where(kind == 0, BLOCK, row + 1) + (stretch - base) * BLOCK
    bottom = (low - base) * BLOCK
    column = lax.broadcasted_iota(jnp.int32, (BLOCK, CHUNK), 1)

    def block(ref, chunk):
        return ref[pl.ds(base + 2 * chunk, 2)].reshape(CHUNK, HEAD_DIM)

    largest = None
    for chunk in range(chunks):
        score = matmul(query, block(keys, chunk), 1, 1)
        place = column + chunk * CHUNK
        score = jnp.where((place >= bottom) & (place < top), score, -1e30)
        scores[:, pl.ds(chunk * CHUNK, CHUNK)] = score
        grads[:, pl.ds(chunk * CHUNK, CHUNK)] = matmul(out_grad, block(values, chunk), 1, 1)
        largest = score if largest is None else jnp.maximum(largest, score)
    largest = jnp.max(largest, axis=1, keepdims=True)

    total = None
    for chunk in range(chunks):
        weight = jnp.exp((scores[:, pl.ds(chunk * CHUNK, CHUNK)] - largest) * SCALE)
        scores[:, pl.ds(chunk * CHUNK, CHUNK)] = weight
        total = weight if total is None else total + weight
    inverse = 1.0 / jnp.sum(total, axis=1, keepdims=True)

    attended = None
    for chunk in range(chunks):
        weight = scores[:, pl.ds(chunk * CHUNK, CHUNK)] * inverse
        scores[:, pl.ds(chunk * CHUNK, CHUNK)] = weight
        rounded = weight.astype(jnp.bfloat16)
        part = matmul(rounded, block(values, chunk), 1, 0)
        attended = part if attended is None else attended + part
        term = matmul(out_grad, rounded, 0, 0)
        value_acc[base + 2 * chunk] += term[:, :BLOCK]
        value_acc[base + 2 * chunk + 1] += term[:, BLOCK:]
    attended = attended.astype(jnp.bfloat16)
    grad_dot = jnp.sum(
        out_grad.astype(jnp.float32) * attended.astype(jnp.float32), axis=1, keepdims=True
    )

    query_grad = None
    for chunk in range(chunks):
        here = pl.ds(chunk * CHUNK, CHUNK)
        score_grad = (scores[:, here] * (grads[:, here] - grad_dot)).astype(jnp.bfloat16)
        part = matmul(score_grad, block(keys, chunk), 1, 0)
        query_grad = part if query_grad is None else query_grad + part
        term = matmul(query, score_grad, 0, 0)
        key_acc[base + 2 * chunk] += term[:, :BLOCK]
        key_acc[base + 2 * chunk + 1] += term[:, BLOCK:]
    query_grad = (query_grad * SCALE).astype(jnp.bfloat16)

    pieces = BLOCK // PIECE
    out[pl.ds(slot * pieces, pieces), 0] = attended.reshape(pieces, PIECE, HEAD_DIM)
    out[pl.ds(slot * pieces, pieces), 1] = query_grad.reshape(pieces, PIECE, HEAD_DIM)


def attend_kernel(
    window_of,
    slot_stretch,
    doc_id,
    diag_kind,
    given,
    out,
    keys,
    values,
    key_acc,
    value_acc,
    scores,
    grads,
    slot_of,
):
    window = window_of()
    first = window * WIN

    for slot in range(WIN):
        stretch = slot_stretch[first + slot] - first
        slot_of[stretch] = slot
        keys[stretch] = given[1, slot]
        values[stretch] = given[2, slot]
    key_acc[...] = jnp.zeros_like(key_acc)
    value_acc[...] = jnp.zeros_like(value_acc)
    refs = (given, out, keys, values, key_acc, value_acc, scores, grads)

    def one(stretch, carry):
        slot = slot_of[stretch]
        low = doc_id[first + stretch] - first
        kind = diag_kind[first + stretch]
        count = stretch + 1 - low
        least = 0
        for width in (256, 512, 1024, 2048):
            most = width // BLOCK

            @pl.when((count > least) & (count <= most))
            def _(width=width):
                attend_tile(width, stretch, slot, low, kind, refs)

            least = most
        return carry

    lax.fori_loop(0, WIN, one, 0)

    pieces = BLOCK // PIECE

    def finish(stretch, carry):
        slot = slot_of[stretch]
        key_grad = (key_acc[stretch] * SCALE).T.astype(jnp.bfloat16)
        value_grad = value_acc[stretch].T.astype(jnp.bfloat16)
        out[pl.ds(slot * pieces, pieces), 2] = key_grad.reshape(pieces, PIECE, HEAD_DIM)
        out[pl.ds(slot * pieces, pieces), 3] = value_grad.reshape(pieces, PIECE, HEAD_DIM)
        return carry

    lax.fori_loop(0, WIN, finish, 0)


def attend(given, slot_stretch, doc_id, diag_kind, window_of):
    whole = pl.BlockSpec(memory_space=pltpu.VMEM)
    scalars = pl.BlockSpec(memory_space=pltpu.SMEM)
    return pl.pallas_call(
        functools.partial(attend_kernel, window_of),
        name="attend_head",
        out_shape=jax.ShapeDtypeStruct((PIECES, ARRAYS, PIECE, HEAD_DIM), jnp.bfloat16),
        in_specs=[scalars, scalars, scalars, whole],
        out_specs=whole,
        scratch_shapes=[
            pltpu.VMEM((WIN, BLOCK, HEAD_DIM), jnp.bfloat16),
            pltpu.VMEM((WIN, BLOCK, HEAD_DIM), jnp.bfloat16),
            pltpu.VMEM((WIN, HEAD_DIM, BLOCK), jnp.float32),
            pltpu.VMEM((WIN, HEAD_DIM, BLOCK), jnp.float32),
            pltpu.VMEM((BLOCK, WIN * BLOCK), jnp.float32),
            pltpu.VMEM((BLOCK, WIN * BLOCK), jnp.float32),
            pltpu.SMEM((WIN,), jnp.int32),
        ],
        compiler_params=pltpu.CompilerParams(vmem_limit_bytes=48 * 1024 * 1024),
    )(slot_stretch, doc_id, diag_kind, given)


def collect_kernel(made, landed, send_sem, recv_sem, own_sem):
    cp, hp = lax.axis_index("cp"), lax.axis_index("hp")
    member = lax.rem(cp, GROUP)
    first = cp - member
    owner = is_owner(member)
    head = hp * HEADS_HERE + head_of(member)
    me = member * HP + hp

    barrier = pltpu.get_barrier_semaphore()

    def greet(step, carry):
        peer = lax.rem(me + step, PIECES)
        peer_member, peer_hp = peer // HP, lax.rem(peer, HP)

        @pl.when(is_owner(peer_member))
        def _():
            pl.semaphore_signal(
                barrier, inc=1, device_id=(first + peer_member, peer_hp), device_id_type=MESH
            )

        return carry

    lax.fori_loop(1, PIECES, greet, 0)

    def copy_to(step):
        peer = lax.rem(me + PIECES // 2 + step, PIECES)
        peer_member, peer_hp = peer // HP, lax.rem(peer, HP)
        return peer, pltpu.make_async_remote_copy(
            src_ref=made.at[peer],
            dst_ref=landed.at[head],
            send_sem=send_sem.at[step],
            recv_sem=recv_sem.at[head],
            device_id=(first + peer_member, peer_hp),
            device_id_type=MESH,
        )

    @pl.when(owner)
    def _():
        pl.semaphore_wait(barrier, PIECES - 1)

        def send(step, carry):
            peer, copy = copy_to(step)

            @pl.when(peer != me)
            def _():
                copy.start()

            return carry

        lax.fori_loop(0, PIECES, send, 0)
        pltpu.make_async_copy(made.at[me], landed.at[head], own_sem).start()

        def sent(step, carry):
            peer, copy = copy_to(step)

            @pl.when(peer != me)
            def _():
                copy.wait_send()

            return carry

        lax.fori_loop(0, PIECES, sent, 0)
        pltpu.make_async_copy(made.at[me], landed.at[head], own_sem).wait()

    def arrived(index, carry):
        @pl.when((index != head) | jnp.logical_not(owner))
        def _():
            pltpu.make_async_copy(landed.at[index], landed.at[index], recv_sem.at[index]).wait()

        return carry

    lax.fori_loop(0, HP * HEADS_HERE, arrived, 0)


def collect(made):
    heads = HP * HEADS_HERE
    return pl.pallas_call(
        collect_kernel,
        name="collect_heads",
        out_shape=jax.ShapeDtypeStruct((heads, ARRAYS, PIECE, HEAD_DIM), jnp.bfloat16),
        in_specs=[pl.BlockSpec(memory_space=pl.ANY)],
        out_specs=pl.BlockSpec(memory_space=pl.ANY),
        scratch_shapes=[
            pltpu.SemaphoreType.DMA((PIECES,)),
            pltpu.SemaphoreType.DMA((heads,)),
            pltpu.SemaphoreType.DMA,
        ],
        compiler_params=pltpu.CompilerParams(collective_id=1, has_side_effects=True),
    )(made)


def rows_kernel(landed, *outs):
    for array, out in enumerate(outs):
        for head in range(HP * HEADS_HERE):
            out[:, head * HEAD_DIM : (head + 1) * HEAD_DIM] = landed[head, array]


def rows(landed):
    whole = pl.BlockSpec(memory_space=pltpu.VMEM)
    shape = jax.ShapeDtypeStruct((PIECE, HP * HEADS_HERE * HEAD_DIM), jnp.bfloat16)
    return pl.pallas_call(
        rows_kernel,
        name="heads_to_rows",
        out_shape=[shape] * ARRAYS,
        in_specs=[whole],
        out_specs=[whole] * ARRAYS,
        compiler_params=pltpu.CompilerParams(vmem_limit_bytes=32 * 1024 * 1024),
    )(landed)


def body(queries, key_rows, value_rows, out_grad, slot_stretch, doc_id, diag_kind):
    landed = spread((queries, key_rows, value_rows, out_grad))
    made = attend(
        landed.reshape(ARRAYS, WIN, BLOCK, HEAD_DIM),
        slot_stretch,
        doc_id,
        diag_kind,
        lambda: lax.axis_index("cp") // GROUP,
    )
    return tuple(rows(collect(made)))


def solution(mesh):
    in_specs = (P("cp", "hp"), P("cp", "hp"), P("cp", "hp"), P("cp", "hp"), P(), P(), P())
    out_specs = (P(("cp", "hp"), None),) * 4
    return jax.shard_map(body, mesh=mesh, in_specs=in_specs, out_specs=out_specs, check_vma=False)
```

time: 490 us -> 109 us (0.22)
  waiting for transfers between devices: 300 us -> 0 us
  Pallas kernels: 0 us -> 104 us
  starting transfers between devices: 51.3 us -> 0 us
  matrix products: 49.7 us -> 0 us
  other arithmetic: 48.7 us -> 0 us
  local copies, waits for them, and re-layouts: 30 us -> 4.33 us
    ppermute x12 -> x0, waiting for transfers between devices: 286 us -> none  [swapped(): lax.ppermute(array, axis, [(i, i ^ 1 << apart) for i in range(lax.axis_si...]
    pallas_call x0 -> x4, Pallas kernels: none -> 104 us  [the longest x1 47.4 us: collect(): pl.pallas_call(collect_kernel, name='collect_heads', out_shape=jax.ShapeD...]
    dot_general x36 -> x0, matrix products: 49.7 us -> none  [the longest x6 12.6 us: query_side(): jnp.dot(score_grad, head_keys, preferred_element_type=jnp.float32)]
    ppermute x12 -> x0, starting transfers between devices: 36.3 us -> none  [swapped(): lax.ppermute(array, axis, [(i, i ^ 1 << apart) for i in range(lax.axis_si...]
    select_n x12 -> x0, other arithmetic: 19.9 us -> none  [the longest x6 13.9 us: join_pair(): jnp.where(upper_bit == 1, jnp.concatenate([arrived, holding], axis_dim),...]
    reduce_sum x25 -> x0, other arithmetic: 16 us -> none  [the longest x6 5.74 us: query_side(): jnp.sum(head_grads.astype(jnp.float32) * attended.astype(jnp.float32), ax...]
    all_to_all x4 -> x0, starting transfers between devices: 15 us -> none  [the longest x1 4.03 us: body(): lax.all_to_all(heads_to_rows(attended), 'hp', split_axis=0, concat_axis=1...]
    all_to_all x4 -> x0, waiting for transfers between devices: 14.1 us -> none  [the longest x1 5.26 us: body(): lax.all_to_all(heads_to_rows(attended), 'hp', split_axis=0, concat_axis=1...]
  transfers between devices with their start and end apart: 16 -> 0, of which waited for: 11 -> 0; matrix products, arithmetic and copies ran while one was open for 5% -> 0% of each run, Pallas kernels for 0% -> 0%
where the time goes in v1:
time: 109 us
  Pallas kernels  104 us (95%)
  local copies, waits for them, and re-layouts  4.33 us (4%)
    pallas_call x1, Pallas kernels, collect(): pl.pallas_call(collect_kernel, name='collect_heads', out_shape=jax.ShapeD...  47.4 us
    pallas_call x1, Pallas kernels, spread(): pl.pallas_call(spread_kernel, name='spread_heads', out_shape=jax.ShapeDty...  37 us
    pallas_call x1, Pallas kernels, attend(): pl.pallas_call(functools.partial(attend_kernel, window_of), name='attend_...  18.2 us
    unnamed x12, local copies, waits for them, and re-layouts  4.33 us

profile of v1, /device:TPU:1, one launch (start us, length us, event | category | flops | bytes accessed | tf_op | source)
XLA Modules:
  0.0 109.1 jit_solution(6754365735483875391)
XLA Ops:
  0.6 0.0 copy-start.5
  0.6 0.0 copy-start.4
  0.7 0.0 copy-start.3
  0.7 37.0 %spread_heads.1 = bf16[4,2048,128]{2,1,0:T(8,128)(2,1)} custom-call(bf16[256,768]{1,0:T(8,128)(2,1)} %refs_0_.1, bf16[256,768]{1,0:T(8,128)(2,1)} %refs_1_.1, bf16[256,768]{1,0:T(8,128)(2,1)} %refs_2_.1, bf16[256,768]{1,0:T(8,128)(2,1)} %refs_3_.1), custom_call_target="tpu_custom_call" | custom-call | tf_op jit(solution)/shard_map/spread_heads/pallas_call | solution.py:107
  37.7 0.0 copy-done.5
  37.7 0.0 copy-done.4
  37.7 0.0 copy-done.3
  37.7 0.0 copy-start.1
  37.8 1.6 %copy-done.1 = bf16[4,2048,128]{2,1,0:T(8,128)(2,1)S(1)} copy-done((bf16[4,2048,128]{2,1,0:T(8,128)(2,1)S(1)}, bf16[4,2048,128]{2,1,0:T(8,128)(2,1)}, u32[]{:S(2)}) %copy-start.1) | copy-done | bytes 2097176
  39.3 18.2 %attend_head.1.made = bf16[32,4,64,128]{3,2,1,0:T(8,128)(2,1)S(1)} custom-call(s32[256]{0:T(256)S(1)} %copy-done.3, s32[256]{0:T(256)S(1)} %copy-done.4, s32[256]{0:T(256)S(1)} %copy-done.5, bf16[4,16,128,128]{3,2,1,0:T(8,128)(2,1)S(1)} %bitcast.1), custom_call_target="tpu_custom_call" | custom-call | tf_op jit(solution)/shard_map/attend_head/pallas_call | solution.py:249
  57.6 0.0 copy-start
  57.6 1.3 %copy-done = bf16[32,4,64,128]{3,2,1,0:T(8,128)(2,1)} copy-done((bf16[32,4,64,128]{3,2,1,0:T(8,128)(2,1)}, bf16[32,4,64,128]{3,2,1,0:T(8,128)(2,1)S(1)}, u32[]{:S(2)}) %copy-start) | copy-done | bytes 2097176
  58.9 47.4 %collect_heads.1.landed = bf16[24,4,64,128]{3,2,1,0:T(8,128)(2,1)} custom-call(bf16[32,4,64,128]{3,2,1,0:T(8,128)(2,1)} %copy-done), custom_call_target="tpu_custom_call" | custom-call | tf_op jit(solution)/shard_map/collect_heads/pallas_call | solution.py:344
  106.3 0.0 copy-start.2
  106.3 1.4 %copy-done.2 = bf16[24,4,64,128]{3,2,1,0:T(8,128)(2,1)S(1)} copy-done((bf16[24,4,64,128]{3,2,1,0:T(8,128)(2,1)S(1)}, bf16[24,4,64,128]{3,2,1,0:T(8,128)(2,1)}, u32[]{:S(2)}) %copy-start.2) | copy-done | bytes 1572888
  107.7 1.4 %heads_to_rows.1 = (bf16[64,3072]{1,0:T(8,128)(2,1)}, bf16[64,3072]{1,0:T(8,128)(2,1)}, bf16[64,3072]{1,0:T(8,128)(2,1)}, bf16[64,3072]{1,0:T(8,128)(2,1)}) custom-call(bf16[24,4,64,128]{3,2,1,0:T(8,128)(2,1)S(1)} %copy-done.2), custom_call_target="tpu_custom_call" | custom-call | tf_op jit(solution)/shard_map/heads_to_rows/pallas_call | solution.py:368
Async XLA Ops:
  0.6 37.1 %copy-start.5 = (s32[256]{0:T(256)S(1)}, s32[256]{0:T(256)}, u32[]{:S(2)}) copy-start(s32[256]{0:T(256)} %diag_kind.1) | copy-start | bytes 3076
  0.6 37.1 %copy-start.4 = (s32[256]{0:T(256)S(1)}, s32[256]{0:T(256)}, u32[]{:S(2)}) copy-start(s32[256]{0:T(256)} %doc_id.1) | copy-start | bytes 3076
  0.7 37.1 %copy-start.3 = (s32[256]{0:T(256)S(1)}, s32[256]{0:T(256)}, u32[]{:S(2)}) copy-start(s32[256]{0:T(256)} %slot_stretch.1) | copy-start | bytes 3076
  37.7 1.6 %copy-start.1 = (bf16[4,2048,128]{2,1,0:T(8,128)(2,1)S(1)}, bf16[4,2048,128]{2,1,0:T(8,128)(2,1)}, u32[]{:S(2)}) copy-start(bf16[4,2048,128]{2,1,0:T(8,128)(2,1)} %spread_heads.1) | copy-start | bytes 6291460
  57.6 1.3 %copy-start = (bf16[32,4,64,128]{3,2,1,0:T(8,128)(2,1)}, bf16[32,4,64,128]{3,2,1,0:T(8,128)(2,1)S(1)}, u32[]{:S(2)}) copy-start(bf16[32,4,64,128]{3,2,1,0:T(8,128)(2,1)S(1)} %attend_head.1.made) | copy-start | bytes 6291460
  106.3 1.4 %copy-start.2 = (bf16[24,4,64,128]{3,2,1,0:T(8,128)(2,1)S(1)}, bf16[24,4,64,128]{3,2,1,0:T(8,128)(2,1)}, u32[]{:S(2)}) copy-start(bf16[24,4,64,128]{3,2,1,0:T(8,128)(2,1)} %collect_heads.1.landed) | copy-start | bytes 4718596

commit v2 on v0

v2 whole, which is shorter than its diff:
```python
import math

import jax
import jax.numpy as jnp
from jax import lax
from jax.experimental import pallas as pl
from jax.experimental.pallas import tpu as pltpu
from jax.sharding import PartitionSpec as P

HEAD_DIM = 128
BLOCK = 128
WIN = 16
ROWS = WIN * BLOCK
GROUP = 8
OWN_SLOTS = WIN // GROUP
HEADS_HERE = 6
HP = 4
PIECES = GROUP * HP
PIECE = ROWS // PIECES
ARRAYS = 4
CHUNK = 256
STEP = 4
MESH = pl.DeviceIdType.MESH
SCALE = 1.0 / math.sqrt(HEAD_DIM)


def owner_of(head):
    return head + jnp.where(head >= 1, 1, 0) + jnp.where(head >= 5, 1, 0)


def head_of(member):
    return member - jnp.where(member >= 2, 1, 0) - jnp.where(member >= 7, 1, 0)


def is_owner(member):
    return (member != 1) & (member != 6)


def matmul(left, right, left_dim, right_dim):
    return lax.dot_general(
        left, right, (((left_dim,), (right_dim,)), ((), ())), preferred_element_type=jnp.float32
    )


def block_rows(index):
    return pl.ds(pl.multiple_of(index * BLOCK, BLOCK), BLOCK)


def in_order(given, slot_of, ordered, turned):
    for stretch in range(WIN):
        here = pl.ds(stretch * BLOCK, BLOCK)
        block = given[slot_of[stretch]]
        ordered[here] = block
        if turned is not None:
            turned[:, here] = block.T


def to_slots(ordered, stretch_of, staged, array):
    for slot in range(WIN):
        staged[array, pl.ds(slot * BLOCK, BLOCK)] = ordered[stretch_of[slot]]


def by_rows(one):
    for band in range(WIN // STEP):

        def step(stretch, carry, band=band):
            one(stretch, (band + 1) * STEP * BLOCK)
            return carry

        lax.fori_loop(band * STEP, (band + 1) * STEP, step, 0)


def kernel(
    slot_stretch,
    doc_id,
    diag_kind,
    queries,
    key_rows,
    value_rows,
    out_grad,
    attended_out,
    query_out,
    key_out,
    value_out,
    given_queries,
    given_keys,
    given_values,
    given_grads,
    staged,
    query,
    key,
    value,
    grad,
    query_turned,
    grad_turned,
    attended,
    result,
    weights,
    score_grads,
    scores,
    give_sem,
    given_sem,
    send_sem,
    out_sem,
):
    sources = (queries, key_rows, value_rows, out_grad)
    given = (given_queries, given_keys, given_values, given_grads)
    outs = (attended_out, query_out, key_out, value_out)
    cp, hp = lax.axis_index("cp"), lax.axis_index("hp")
    member = lax.rem(cp, GROUP)
    first = cp - member
    owner = is_owner(member)
    own_head = head_of(member)
    me = member * HP + hp

    barrier = pltpu.get_barrier_semaphore()

    def greet(step, carry):
        peer = lax.rem(me + step, PIECES)
        peer_member, peer_hp = peer // HP, lax.rem(peer, HP)

        @pl.when(is_owner(peer_member) | (owner & (peer_hp == hp)))
        def _():
            pl.semaphore_signal(
                barrier, inc=1, device_id=(first + peer_member, peer_hp), device_id_type=MESH
            )

        return carry

    lax.fori_loop(1, PIECES, greet, 0)
    pl.semaphore_wait(barrier, jnp.where(owner, PIECES - 1, HEADS_HERE))

    own_slots = pl.ds(member * OWN_SLOTS, OWN_SLOTS)

    def give(array, step):
        head = jnp.where(member < GROUP // 2, HEADS_HERE - 1 - step, step)
        target = owner_of(head)
        columns = pl.ds(pl.multiple_of(head * HEAD_DIM, HEAD_DIM), HEAD_DIM)
        return target, pltpu.make_async_remote_copy(
            src_ref=sources[array].at[:, :, columns],
            dst_ref=given[array].at[own_slots],
            send_sem=give_sem.at[array, step],
            recv_sem=given_sem.at[array],
            device_id=(first + target, hp),
            device_id_type=MESH,
        )

    for array in range(ARRAYS):
        for step in range(HEADS_HERE):
            target, copy = give(array, step)

            @pl.when(target != member)
            def _(copy=copy):
                copy.start()

        @pl.when(owner)
        def _(array=array):
            columns = pl.ds(pl.multiple_of(own_head * HEAD_DIM, HEAD_DIM), HEAD_DIM)
            pltpu.make_async_copy(
                sources[array].at[:, :, columns], given[array].at[own_slots], given_sem.at[array]
            ).start()

    def arrived(array):
        pltpu.make_async_copy(given[array], given[array], given_sem.at[array]).wait()

    def out_columns():
        return pl.ds(
            pl.multiple_of((hp * HEADS_HERE + own_head) * HEAD_DIM, HEAD_DIM), HEAD_DIM
        )

    def piece_rows(piece):
        return pl.ds(pl.multiple_of(piece * PIECE, PIECE), PIECE)

    def send(array):
        def one(step, carry):
            peer = lax.rem(me + PIECES // 2 + step, PIECES)
            peer_member, peer_hp = peer // HP, lax.rem(peer, HP)

            @pl.when(peer != me)
            def _():
                pltpu.make_async_remote_copy(
                    src_ref=staged.at[array, piece_rows(peer)],
                    dst_ref=outs[array].at[:, out_columns()],
                    send_sem=send_sem.at[array],
                    recv_sem=out_sem.at[array],
                    device_id=(first + peer_member, peer_hp),
                    device_id_type=MESH,
                ).start()

            return carry

        lax.fori_loop(0, PIECES, one, 0)
        pltpu.make_async_copy(
            staged.at[array, piece_rows(me)], outs[array].at[:, out_columns()], out_sem.at[array]
        ).start()

    @pl.when(owner)
    def _():
        base = (first // GROUP) * WIN
        stretch_of = [lax.rem(slot_stretch[base + slot], WIN) for slot in range(WIN)]
        slot_of = []
        for stretch in range(WIN):
            place = jnp.int32(0)
            for slot in range(1, WIN):
                place = jnp.where(stretch_of[slot] == stretch, slot, place)
            slot_of.append(place)

        arrived(0)
        in_order(given[0], slot_of, query, query_turned)
        arrived(1)
        in_order(given[1], slot_of, key, None)

        row = lax.broadcasted_iota(jnp.int32, (BLOCK, 1), 0)
        column = lax.broadcasted_iota(jnp.int32, (BLOCK, CHUNK), 1)

        def weigh(stretch, width):
            here = block_rows(stretch)
            bottom = (doc_id[base + stretch] - base) * BLOCK
            top = jnp.where(diag_kind[base + stretch] == 0, BLOCK, row + 1) + stretch * BLOCK
            own = query[here]
            largest = None
            for start in range(0, width, CHUNK):
                score = matmul(own, key[pl.ds(start, CHUNK)], 1, 1)
                place = column + start
                score = jnp.where((place >= bottom) & (place < top), score, -1e30)
                scores[:, pl.ds(start, CHUNK)] = score
                largest = score if largest is None else jnp.maximum(largest, score)
            largest = jnp.max(largest, axis=1, keepdims=True)
            total = None
            for start in range(0, width, CHUNK):
                weight = jnp.exp((scores[:, pl.ds(start, CHUNK)] - largest) * SCALE)
                scores[:, pl.ds(start, CHUNK)] = weight
                total = weight if total is None else total + weight
            inverse = 1.0 / jnp.sum(total, axis=1, keepdims=True)
            for start in range(0, width, CHUNK):
                weight = scores[:, pl.ds(start, CHUNK)] * inverse
                weights[here, pl.ds(start, CHUNK)] = weight.astype(jnp.bfloat16)

        by_rows(weigh)

        arrived(2)
        in_order(given[2], slot_of, value, None)

        def forward(stretch, width):
            here = block_rows(stretch)
            attended[stretch] = matmul(
                weights[here, pl.ds(0, width)], value[pl.ds(0, width)], 1, 0
            ).astype(jnp.bfloat16)

        by_rows(forward)
        to_slots(attended, stretch_of, staged, 0)
        send(0)

        arrived(3)
        in_order(given[3], slot_of, grad, grad_turned)

        def over_queries(turned, pairs, factor):
            for start in range(0, ROWS, CHUNK):
                rest = pl.ds(start, ROWS - start)
                here = pl.ds(start, CHUNK)
                term = matmul(turned[:, rest], pairs[rest, here], 1, 0)
                if factor is not None:
                    term = term * factor
                turned_back = term.T.astype(jnp.bfloat16)
                result[start // BLOCK] = turned_back[:BLOCK]
                result[start // BLOCK + 1] = turned_back[BLOCK:]

        over_queries(grad_turned, weights, None)
        to_slots(result, stretch_of, staged, 3)
        send(3)

        def backward(stretch, width):
            here = block_rows(stretch)
            own = grad[here]
            grad_dot = jnp.sum(
                own.astype(jnp.float32) * attended[stretch].astype(jnp.float32), axis=1, keepdims=True
            )
            for start in range(0, width, CHUNK):
                columns = pl.ds(start, CHUNK)
                weight_grad = matmul(own, value[columns], 1, 1)
                weight = weights[here, columns].astype(jnp.float32)
                score_grads[here, columns] = (weight * (weight_grad - grad_dot)).astype(
                    jnp.bfloat16
                )
            query_grad = matmul(score_grads[here, pl.ds(0, width)], key[pl.ds(0, width)], 1, 0)
            result[stretch] = (query_grad * SCALE).astype(jnp.bfloat16)

        by_rows(backward)
        to_slots(result, stretch_of, staged, 1)
        send(1)

        over_queries(query_turned, score_grads, SCALE)
        to_slots(result, stretch_of, staged, 2)
        send(2)

    for array in range(ARRAYS):
        for step in range(HEADS_HERE):
            target, copy = give(array, step)

            @pl.when(target != member)
            def _(copy=copy):
                copy.wait_send()

    @pl.when(owner)
    def _():
        for array in range(ARRAYS):
            gone = staged.at[array, pl.ds(0, ROWS - PIECE)]
            pltpu.make_async_copy(gone, gone, send_sem.at[array]).wait()

    for array in range(ARRAYS):
        pltpu.make_async_copy(outs[array], outs[array], out_sem.at[array]).wait()


def body(queries, key_rows, value_rows, out_grad, slot_stretch, doc_id, diag_kind):
    anywhere = pl.BlockSpec(memory_space=pl.ANY)
    scalars = pl.BlockSpec(memory_space=pltpu.SMEM)
    shape = jax.ShapeDtypeStruct((PIECE, HP * HEADS_HERE * HEAD_DIM), jnp.bfloat16)
    ordered = pltpu.VMEM((ROWS, HEAD_DIM), jnp.bfloat16)
    stacked = pltpu.VMEM((WIN, BLOCK, HEAD_DIM), jnp.bfloat16)
    turned = pltpu.VMEM((HEAD_DIM, ROWS), jnp.bfloat16)
    pairs = pltpu.VMEM((ROWS, ROWS), jnp.bfloat16)
    arrays = [
        array.reshape(OWN_SLOTS, BLOCK, HEADS_HERE * HEAD_DIM)
        for array in (queries, key_rows, value_rows, out_grad)
    ]
    return tuple(
        pl.pallas_call(
            kernel,
            name="attend_windows",
            out_shape=[shape] * ARRAYS,
            in_specs=[scalars] * 3 + [anywhere] * ARRAYS,
            out_specs=[anywhere] * ARRAYS,
            scratch_shapes=[
                stacked,
                stacked,
                stacked,
                stacked,
                pltpu.VMEM((ARRAYS, ROWS, HEAD_DIM), jnp.bfloat16),
                ordered,
                ordered,
                ordered,
                ordered,
                turned,
                turned,
                stacked,
                stacked,
                pairs,
                pairs,
                pltpu.VMEM((BLOCK, ROWS), jnp.float32),
                pltpu.SemaphoreType.DMA((ARRAYS, HEADS_HERE)),
                pltpu.SemaphoreType.DMA((ARRAYS,)),
                pltpu.SemaphoreType.DMA((ARRAYS,)),
                pltpu.SemaphoreType.DMA((ARRAYS,)),
            ],
            compiler_params=pltpu.CompilerParams(
                collective_id=0, has_side_effects=True, vmem_limit_bytes=48 * 1024 * 1024
            ),
        )(slot_stretch, doc_id, diag_kind, *arrays)
    )


def solution(mesh):
    in_specs = (P("cp", "hp"), P("cp", "hp"), P("cp", "hp"), P("cp", "hp"), P(), P(), P())
    out_specs = (P(("cp", "hp"), None),) * 4
    return jax.shard_map(body, mesh=mesh, in_specs=in_specs, out_specs=out_specs, check_vma=False)
```

time: 490 us -> 88.3 us (0.18)
  waiting for transfers between devices: 300 us -> 0 us
  Pallas kernels: 0 us -> 79.7 us
  starting transfers between devices: 51.3 us -> 0 us
  matrix products: 49.7 us -> 0 us
  other arithmetic: 48.7 us -> 0 us
  local copies, waits for them, and re-layouts: 30 us -> 7.65 us
    ppermute x12 -> x0, waiting for transfers between devices: 286 us -> none  [swapped(): lax.ppermute(array, axis, [(i, i ^ 1 << apart) for i in range(lax.axis_si...]
    pallas_call x0 -> x1, Pallas kernels: none -> 79.7 us  [body(): pl.pallas_call(kernel, name='attend_windows', out_shape=[shape] * ARRAYS,...]
    dot_general x36 -> x0, matrix products: 49.7 us -> none  [the longest x6 12.6 us: query_side(): jnp.dot(score_grad, head_keys, preferred_element_type=jnp.float32)]
    ppermute x12 -> x0, starting transfers between devices: 36.3 us -> none  [swapped(): lax.ppermute(array, axis, [(i, i ^ 1 << apart) for i in range(lax.axis_si...]
    select_n x12 -> x0, other arithmetic: 19.9 us -> none  [the longest x6 13.9 us: join_pair(): jnp.where(upper_bit == 1, jnp.concatenate([arrived, holding], axis_dim),...]
    reduce_sum x25 -> x0, other arithmetic: 16 us -> none  [the longest x6 5.74 us: query_side(): jnp.sum(head_grads.astype(jnp.float32) * attended.astype(jnp.float32), ax...]
    all_to_all x4 -> x0, starting transfers between devices: 15 us -> none  [the longest x1 4.03 us: body(): lax.all_to_all(heads_to_rows(attended), 'hp', split_axis=0, concat_axis=1...]
    all_to_all x4 -> x0, waiting for transfers between devices: 14.1 us -> none  [the longest x1 5.26 us: body(): lax.all_to_all(heads_to_rows(attended), 'hp', split_axis=0, concat_axis=1...]
  transfers between devices with their start and end apart: 16 -> 0, of which waited for: 11 -> 0; matrix products, arithmetic and copies ran while one was open for 5% -> 0% of each run, Pallas kernels for 0% -> 0%
where the time goes in v2:
time: 88.3 us; the launch traced here: 88 us
  Pallas kernels  79.7 us (90%)
  local copies, waits for them, and re-layouts  7.65 us (9%)
    pallas_call x1, Pallas kernels, body(): pl.pallas_call(kernel, name='attend_windows', out_shape=[shape] * ARRAYS,...  79.7 us
    unnamed x18, local copies, waits for them, and re-layouts  7.65 us

profile of v2, /device:TPU:1, one launch (start us, length us, event | category | flops | bytes accessed | tf_op | source)
XLA Modules:
  0.0 88.0 jit_solution(3277324493363108113)
XLA Ops:
  0.6 0.0 copy-start.5
  0.6 0.0 copy-start.6
  0.7 0.0 copy-start.4
  0.7 0.7 copy-done.5
  1.3 0.0 copy-done.6
  1.3 0.0 copy-done.4
  1.3 0.0 copy-start
  1.3 1.0 %copy-done = bf16[256,768]{1,0:T(8,128)(2,1)S(1)} copy-done((bf16[256,768]{1,0:T(8,128)(2,1)S(1)}, bf16[256,768]{1,0:T(8,128)(2,1)}, u32[]{:S(2)}) %copy-start) | copy-done | bytes 393240
  2.3 0.0 copy-start.1
  2.3 1.0 %copy-done.1 = bf16[256,768]{1,0:T(8,128)(2,1)S(1)} copy-done((bf16[256,768]{1,0:T(8,128)(2,1)S(1)}, bf16[256,768]{1,0:T(8,128)(2,1)}, u32[]{:S(2)}) %copy-start.1) | copy-done | bytes 393240
  3.3 0.0 copy-start.2
  3.3 1.0 %copy-done.2 = bf16[256,768]{1,0:T(8,128)(2,1)S(1)} copy-done((bf16[256,768]{1,0:T(8,128)(2,1)S(1)}, bf16[256,768]{1,0:T(8,128)(2,1)}, u32[]{:S(2)}) %copy-start.2) | copy-done | bytes 393240
  4.3 0.0 copy-start.3
  4.3 1.0 %copy-done.3 = bf16[256,768]{1,0:T(8,128)(2,1)S(1)} copy-done((bf16[256,768]{1,0:T(8,128)(2,1)S(1)}, bf16[256,768]{1,0:T(8,128)(2,1)}, u32[]{:S(2)}) %copy-start.3) | copy-done | bytes 393240
  5.3 79.7 %attend_windows.1 = (bf16[64,3072]{1,0:T(8,128)(2,1)S(1)}, bf16[64,3072]{1,0:T(8,128)(2,1)S(1)}, bf16[64,3072]{1,0:T(8,128)(2,1)S(1)}, bf16[64,3072]{1,0:T(8,128)(2,1)S(1)}) custom-call(s32[256]{0:T(256)S(1)} %copy-done.4, s32[256]{0:T(256)S(1)} %copy-done.5, s32[256]{0:T(256)S(1)} %copy-done.6, bf16[2,128,768]{2,1,0:T(8,128)(2,1)S(1)} %bitcast.4, ...), custom_call_target="tpu_custom_call" | custom-call | tf_op jit(solution)/shard_map/attend_windows/pallas_call | solution.py:327
  85.0 0.7 copy.15
  85.7 0.7 copy.16
  86.5 0.7 copy.17
  87.2 0.7 copy.18
Async XLA Ops:
  0.6 0.7 copy-start.5
  0.6 0.7 copy-start.6
  0.7 0.7 copy-start.4
  1.3 1.0 %copy-start = (bf16[256,768]{1,0:T(8,128)(2,1)S(1)}, bf16[256,768]{1,0:T(8,128)(2,1)}, u32[]{:S(2)}) copy-start(bf16[256,768]{1,0:T(8,128)(2,1)} %param.7) | copy-start | bytes 1179652
  2.3 1.0 %copy-start.1 = (bf16[256,768]{1,0:T(8,128)(2,1)S(1)}, bf16[256,768]{1,0:T(8,128)(2,1)}, u32[]{:S(2)}) copy-start(bf16[256,768]{1,0:T(8,128)(2,1)} %param.8) | copy-start | bytes 1179652
  3.3 1.0 %copy-start.2 = (bf16[256,768]{1,0:T(8,128)(2,1)S(1)}, bf16[256,768]{1,0:T(8,128)(2,1)}, u32[]{:S(2)}) copy-start(bf16[256,768]{1,0:T(8,128)(2,1)} %param.9) | copy-start | bytes 1179652
  4.3 1.0 %copy-start.3 = (bf16[256,768]{1,0:T(8,128)(2,1)S(1)}, bf16[256,768]{1,0:T(8,128)(2,1)}, u32[]{:S(2)}) copy-start(bf16[256,768]{1,0:T(8,128)(2,1)} %param.10) | copy-start | bytes 1179652

commit v3 on v2

--- a/solution.py
+++ b/solution.py
@@ -311,6 +311,42 @@
         pltpu.make_async_copy(outs[array], outs[array], out_sem.at[array]).wait()
 
 
+def settle_kernel(*refs):
+    landed, outs = refs[:ARRAYS], refs[ARRAYS : 2 * ARRAYS]
+    held, in_sems, out_sems = refs[2 * ARRAYS :]
+    coming = [
+        pltpu.make_async_copy(landed[array], held.at[array], in_sems.at[array])
+        for array in range(ARRAYS)
+    ]
+    going = [
+        pltpu.make_async_copy(held.at[array], outs[array], out_sems.at[array])
+        for array in range(ARRAYS)
+    ]
+    for copy in coming:
+        copy.start()
+    for array in range(ARRAYS):
+        coming[array].wait()
+        going[array].start()
+    for copy in going:
+        copy.wait()
+
+
+def settle(landed):
+    anywhere = pl.BlockSpec(memory_space=pl.ANY)
+    return pl.pallas_call(
+        settle_kernel,
+        name="settle_results",
+        out_shape=[jax.ShapeDtypeStruct(array.shape, array.dtype) for array in landed],
+        in_specs=[anywhere] * ARRAYS,
+        out_specs=[anywhere] * ARRAYS,
+        scratch_shapes=[
+            pltpu.VMEM((ARRAYS, *landed[0].shape), jnp.bfloat16),
+            pltpu.SemaphoreType.DMA((ARRAYS,)),
+            pltpu.SemaphoreType.DMA((ARRAYS,)),
+        ],
+    )(*landed)
+
+
 def body(queries, key_rows, value_rows, out_grad, slot_stretch, doc_id, diag_kind):
     anywhere = pl.BlockSpec(memory_space=pl.ANY)
     scalars = pl.BlockSpec(memory_space=pltpu.SMEM)
@@ -323,7 +359,7 @@
         array.reshape(OWN_SLOTS, BLOCK, HEADS_HERE * HEAD_DIM)
         for array in (queries, key_rows, value_rows, out_grad)
     ]
-    return tuple(
+    landed = (
         pl.pallas_call(
             kernel,
             name="attend_windows",
@@ -353,10 +389,11 @@
                 pltpu.SemaphoreType.DMA((ARRAYS,)),
             ],
             compiler_params=pltpu.CompilerParams(
-                collective_id=0, has_side_effects=True, vmem_limit_bytes=48 * 1024 * 1024
+                collective_id=0, has_side_effects=True, vmem_limit_bytes=62 * 1024 * 1024
             ),
         )(slot_stretch, doc_id, diag_kind, *arrays)
     )
+    return tuple(settle(landed))
 
 
 def solution(mesh):

time: 88.3 us -> 83.2 us (0.942)
  local copies, waits for them, and re-layouts: 7.65 us -> 0 us
  Pallas kernels: 79.7 us -> 82.3 us
    unnamed x18 -> x0, local copies, waits for them, and re-layouts: 7.65 us -> none
    pallas_call x0 -> x1, Pallas kernels: none -> 2.2 us  [settle(): pl.pallas_call(settle_kernel, name='settle_results', out_shape=[jax.Shape...]
where the time goes in v3:
time: 83.2 us; the launch traced here: 83 us
  Pallas kernels  82.3 us (99%)
    pallas_call x1, Pallas kernels, body(): pl.pallas_call(kernel, name='attend_windows', out_shape=[shape] * ARRAYS,...  80.1 us
    pallas_call x1, Pallas kernels, settle(): pl.pallas_call(settle_kernel, name='settle_results', out_shape=[jax.Shape...  2.2 us

profile of v3, /device:TPU:1, one launch (start us, length us, event | category | flops | bytes accessed | tf_op | source)
XLA Modules:
  0.0 83.0 jit_solution(4701908788181492798)
XLA Ops:
  0.6 80.1 %attend_windows.1 = (bf16[64,3072]{1,0:T(8,128)(2,1)}, bf16[64,3072]{1,0:T(8,128)(2,1)}, bf16[64,3072]{1,0:T(8,128)(2,1)}, bf16[64,3072]{1,0:T(8,128)(2,1)}) custom-call(s32[256]{0:T(256)} %slot_stretch.1, s32[256]{0:T(256)} %doc_id.1, s32[256]{0:T(256)} %diag_kind.1, bf16[2,128,768]{2,1,0:T(8,128)(2,1)} %bitcast.4, bf16[2,128,768]{2,1,0:T(8,128)(2,1)} %bitcast.5, ...), custom_call_target="tpu_custom_call" | custom-call | tf_op jit(solution)/shard_map/attend_windows/pallas_call | solution.py:363
  80.8 2.2 %settle_results.1 = (bf16[64,3072]{1,0:T(8,128)(2,1)}, bf16[64,3072]{1,0:T(8,128)(2,1)}, bf16[64,3072]{1,0:T(8,128)(2,1)}, bf16[64,3072]{1,0:T(8,128)(2,1)}) custom-call(bf16[64,3072]{1,0:T(8,128)(2,1)} %get-tuple-element.8.refs_0_, bf16[64,3072]{1,0:T(8,128)(2,1)} %get-tuple-element.9.refs_1_, bf16[64,3072]{1,0:T(8,128)(2,1)} %get-tuple-element.10.refs_2_, ...), custom_call_target="tpu_custom_call" | custom-call | tf_op jit(solution)/shard_map/settle_results/pallas_call | solution.py:336

commit v4 on v3

--- a/solution.py
+++ b/solution.py
@@ -102,6 +102,7 @@
     given_sem,
     send_sem,
     out_sem,
+    ready,
 ):
     sources = (queries, key_rows, value_rows, out_grad)
     given = (given_queries, given_keys, given_values, given_grads)
@@ -115,20 +116,26 @@
 
     barrier = pltpu.get_barrier_semaphore()
 
-    def greet(step, carry):
-        peer = lax.rem(me + step, PIECES)
-        peer_member, peer_hp = peer // HP, lax.rem(peer, HP)
-
-        @pl.when(is_owner(peer_member) | (owner & (peer_hp == hp)))
-        def _():
+    for step in range(1, GROUP):
+        peer = lax.rem(member + step, GROUP)
+
+        @pl.when(owner | is_owner(peer))
+        def _(peer=peer):
             pl.semaphore_signal(
-                barrier, inc=1, device_id=(first + peer_member, peer_hp), device_id_type=MESH
+                barrier, inc=1, device_id=(first + peer, hp), device_id_type=MESH
             )
 
-        return carry
-
-    lax.fori_loop(1, PIECES, greet, 0)
-    pl.semaphore_wait(barrier, jnp.where(owner, PIECES - 1, HEADS_HERE))
+    def greet_beside(semaphore):
+        for step in range(1, HP):
+            pl.semaphore_signal(
+                semaphore, inc=1, device_id=(cp, lax.rem(hp + step, HP)), device_id_type=MESH
+            )
+
+    @pl.when(owner)
+    def _():
+        greet_beside(barrier)
+
+    pl.semaphore_wait(barrier, jnp.where(owner, GROUP - 1 + HP - 1, HEADS_HERE))
 
     own_slots = pl.ds(member * OWN_SLOTS, OWN_SLOTS)
 
@@ -160,6 +167,10 @@
                 sources[array].at[:, :, columns], given[array].at[own_slots], given_sem.at[array]
             ).start()
 
+    @pl.when(owner)
+    def _():
+        greet_beside(ready)
+
     def arrived(array):
         pltpu.make_async_copy(given[array], given[array], given_sem.at[array]).wait()
 
@@ -173,8 +184,9 @@
 
     def send(array):
         def one(step, carry):
-            peer = lax.rem(me + PIECES // 2 + step, PIECES)
-            peer_member, peer_hp = peer // HP, lax.rem(peer, HP)
+            peer_member = member ^ (GROUP // 2 ^ step // HP)
+            peer_hp = lax.rem(step, HP)
+            peer = peer_member * HP + peer_hp
 
             @pl.when(peer != me)
             def _():
@@ -249,6 +261,7 @@
 
         by_rows(forward)
         to_slots(attended, stretch_of, staged, 0)
+        pl.semaphore_wait(ready, HP - 1)
         send(0)
 
         arrived(3)
@@ -387,6 +400,7 @@
                 pltpu.SemaphoreType.DMA((ARRAYS,)),
                 pltpu.SemaphoreType.DMA((ARRAYS,)),
                 pltpu.SemaphoreType.DMA((ARRAYS,)),
+                pltpu.SemaphoreType.REGULAR,
             ],
             compiler_params=pltpu.CompilerParams(
                 collective_id=0, has_side_effects=True, vmem_limit_bytes=62 * 1024 * 1024

time: 83.2 us -> 80.6 us (0.969)
  Pallas kernels: 82.3 us -> 79.7 us
    pallas_call x1, Pallas kernels: 80.1 us -> 77.5 us  [body(): pl.pallas_call(kernel, name='attend_windows', out_shape=[shape] * ARRAYS,...]
where the time goes in v4:
time: 80.6 us; the launch traced here: 80.3 us
  Pallas kernels  79.7 us (99%)
    pallas_call x1, Pallas kernels, body(): pl.pallas_call(kernel, name='attend_windows', out_shape=[shape] * ARRAYS,...  77.5 us
    pallas_call x1, Pallas kernels, settle(): pl.pallas_call(settle_kernel, name='settle_results', out_shape=[jax.Shape...  2.2 us

profile of v4, /device:TPU:1, one launch (start us, length us, event | category | flops | bytes accessed | tf_op | source)
XLA Modules:
  0.0 80.3 jit_solution(6338647767438471947)
XLA Ops:
  0.6 77.5 %attend_windows.1 = (bf16[64,3072]{1,0:T(8,128)(2,1)}, bf16[64,3072]{1,0:T(8,128)(2,1)}, bf16[64,3072]{1,0:T(8,128)(2,1)}, bf16[64,3072]{1,0:T(8,128)(2,1)}) custom-call(s32[256]{0:T(256)} %slot_stretch.1, s32[256]{0:T(256)} %doc_id.1, s32[256]{0:T(256)} %diag_kind.1, bf16[2,128,768]{2,1,0:T(8,128)(2,1)} %bitcast.4, bf16[2,128,768]{2,1,0:T(8,128)(2,1)} %bitcast.5, ...), custom_call_target="tpu_custom_call" | custom-call | tf_op jit(solution)/shard_map/attend_windows/pallas_call | solution.py:376
  78.1 2.2 %settle_results.1 = (bf16[64,3072]{1,0:T(8,128)(2,1)}, bf16[64,3072]{1,0:T(8,128)(2,1)}, bf16[64,3072]{1,0:T(8,128)(2,1)}, bf16[64,3072]{1,0:T(8,128)(2,1)}) custom-call(bf16[64,3072]{1,0:T(8,128)(2,1)} %get-tuple-element.8.refs_0_, bf16[64,3072]{1,0:T(8,128)(2,1)} %get-tuple-element.9.refs_1_, bf16[64,3072]{1,0:T(8,128)(2,1)} %get-tuple-element.10.refs_2_, ...), custom_call_target="tpu_custom_call" | custom-call | tf_op jit(solution)/shard_map/settle_results/pallas_call | solution.py:349

commit v5 on v4

--- a/solution.py
+++ b/solution.py
@@ -36,6 +36,10 @@
     return (member != 1) & (member != 6)
 
 
+def rank_of(member):
+    return lax.rem(member + GROUP - 1, GROUP)
+
+
 def matmul(left, right, left_dim, right_dim):
     return lax.dot_general(
         left, right, (((left_dim,), (right_dim,)), ((), ())), preferred_element_type=jnp.float32
@@ -71,9 +75,9 @@
 
 
 def kernel(
-    slot_stretch,
-    doc_id,
-    diag_kind,
+    slot_stretch_whole,
+    doc_id_whole,
+    diag_kind_whole,
     queries,
     key_rows,
     value_rows,
@@ -82,6 +86,9 @@
     query_out,
     key_out,
     value_out,
+    slot_stretch,
+    doc_id,
+    diag_kind,
     given_queries,
     given_keys,
     given_values,
@@ -103,6 +110,9 @@
     send_sem,
     out_sem,
     ready,
+    ready_beside,
+    all_beside,
+    table_sem,
 ):
     sources = (queries, key_rows, value_rows, out_grad)
     given = (given_queries, given_keys, given_values, given_grads)
@@ -114,33 +124,69 @@
     own_head = head_of(member)
     me = member * HP + hp
 
+    tables = [
+        pltpu.make_async_copy(whole, table, table_sem.at[index])
+        for index, (whole, table) in enumerate(
+            (
+                (slot_stretch_whole, slot_stretch),
+                (doc_id_whole, doc_id),
+                (diag_kind_whole, diag_kind),
+            )
+        )
+    ]
+
     barrier = pltpu.get_barrier_semaphore()
+
+    def beside(semaphore, step):
+        pl.semaphore_signal(
+            semaphore, inc=1, device_id=(cp, lax.rem(hp + step, HP)), device_id_type=MESH
+        )
+
+    rank = rank_of(member)
 
     for step in range(1, GROUP):
         peer = lax.rem(member + step, GROUP)
 
-        @pl.when(owner | is_owner(peer))
+        @pl.when((rank_of(peer) > rank) & (owner | is_owner(peer)))
+        def _(peer=peer):
+            pl.semaphore_signal(barrier, inc=1, device_id=(first + peer, hp), device_id_type=MESH)
+
+    for step in range(1, HP):
+
+        @pl.when(owner & (hp + step >= HP))
+        def _(step=step):
+            beside(barrier, step)
+
+    lower_owners = rank - jnp.where(rank > 0, 1, 0)
+    greetings = jnp.where(owner, rank + HP - 1 - hp, lower_owners)
+
+    @pl.when(greetings > 0)
+    def _():
+        pl.semaphore_wait(barrier, greetings)
+
+    for step in range(1, GROUP):
+        peer = lax.rem(member + step, GROUP)
+
+        @pl.when((rank_of(peer) < rank) & (owner | is_owner(peer)))
         def _(peer=peer):
             pl.semaphore_signal(
-                barrier, inc=1, device_id=(first + peer, hp), device_id_type=MESH
+                ready.at[member], inc=1, device_id=(first + peer, hp), device_id_type=MESH
             )
 
-    def greet_beside(semaphore):
-        for step in range(1, HP):
-            pl.semaphore_signal(
-                semaphore, inc=1, device_id=(cp, lax.rem(hp + step, HP)), device_id_type=MESH
-            )
-
-    @pl.when(owner)
-    def _():
-        greet_beside(barrier)
-
-    pl.semaphore_wait(barrier, jnp.where(owner, GROUP - 1 + HP - 1, HEADS_HERE))
+    for step in range(1, HP):
+
+        @pl.when(owner & (hp + step < HP))
+        def _(step=step):
+            beside(ready_beside, step)
 
     own_slots = pl.ds(member * OWN_SLOTS, OWN_SLOTS)
 
     def give(array, step):
-        head = jnp.where(member < GROUP // 2, HEADS_HERE - 1 - step, step)
+        half = HEADS_HERE // 2
+        if step < half:
+            head = jnp.where(member < GROUP // 2, half + step, half - 1 - step)
+        else:
+            head = jnp.where(member < GROUP // 2, HEADS_HERE - 1 - step, step)
         target = owner_of(head)
         columns = pl.ds(pl.multiple_of(head * HEAD_DIM, HEAD_DIM), HEAD_DIM)
         return target, pltpu.make_async_remote_copy(
@@ -156,6 +202,12 @@
         for step in range(HEADS_HERE):
             target, copy = give(array, step)
 
+            if array == 0:
+
+                @pl.when(rank_of(target) > rank)
+                def _(target=target):
+                    pl.semaphore_wait(ready.at[target], 1)
+
             @pl.when(target != member)
             def _(copy=copy):
                 copy.start()
@@ -169,7 +221,23 @@
 
     @pl.when(owner)
     def _():
-        greet_beside(ready)
+        for idle in (1, GROUP - 2):
+
+            @pl.when(rank < idle - 1)
+            def _(idle=idle):
+                pl.semaphore_wait(ready.at[idle], 1)
+
+        @pl.when(hp > 0)
+        def _():
+            pl.semaphore_wait(ready_beside, hp)
+
+        for step in range(1, HP):
+            beside(all_beside, step)
+
+    for table in tables:
+        table.start()
+    for table in tables:
+        table.wait()
 
     def arrived(array):
         pltpu.make_async_copy(given[array], given[array], given_sem.at[array]).wait()
@@ -261,7 +329,7 @@
 
         by_rows(forward)
         to_slots(attended, stretch_of, staged, 0)
-        pl.semaphore_wait(ready, HP - 1)
+        pl.semaphore_wait(all_beside, HP - 1)
         send(0)
 
         arrived(3)
@@ -362,7 +430,6 @@
 
 def body(queries, key_rows, value_rows, out_grad, slot_stretch, doc_id, diag_kind):
     anywhere = pl.BlockSpec(memory_space=pl.ANY)
-    scalars = pl.BlockSpec(memory_space=pltpu.SMEM)
     shape = jax.ShapeDtypeStruct((PIECE, HP * HEADS_HERE * HEAD_DIM), jnp.bfloat16)
     ordered = pltpu.VMEM((ROWS, HEAD_DIM), jnp.bfloat16)
     stacked = pltpu.VMEM((WIN, BLOCK, HEAD_DIM), jnp.bfloat16)
@@ -377,9 +444,10 @@
             kernel,
             name="attend_windows",
             out_shape=[shape] * ARRAYS,
-            in_specs=[scalars] * 3 + [anywhere] * ARRAYS,
+            in_specs=[anywhere] * (3 + ARRAYS),
             out_specs=[anywhere] * ARRAYS,
             scratch_shapes=[
+                *[pltpu.SMEM(table.shape, table.dtype) for table in (slot_stretch, doc_id, diag_kind)],
                 stacked,
                 stacked,
                 stacked,
@@ -400,7 +468,10 @@
                 pltpu.SemaphoreType.DMA((ARRAYS,)),
                 pltpu.SemaphoreType.DMA((ARRAYS,)),
                 pltpu.SemaphoreType.DMA((ARRAYS,)),
+                pltpu.SemaphoreType.REGULAR((GROUP,)),
                 pltpu.SemaphoreType.REGULAR,
+                pltpu.SemaphoreType.REGULAR,
+                pltpu.SemaphoreType.DMA((3,)),
             ],
             compiler_params=pltpu.CompilerParams(
                 collective_id=0, has_side_effects=True, vmem_limit_bytes=62 * 1024 * 1024

time: 80.6 us -> 79.4 us (0.985); the launches traced: 80.3 us -> 77.9 us
  Pallas kernels: 79.7 us -> 77.2 us
    pallas_call x1, Pallas kernels: 77.5 us -> 75 us  [body(): pl.pallas_call(kernel, name='attend_windows', out_shape=[shape] * ARRAYS,...]
where the time goes in v5:
time: 79.4 us; the launch traced here: 77.9 us
  Pallas kernels  77.2 us (97%)
    pallas_call x1, Pallas kernels, body(): pl.pallas_call(kernel, name='attend_windows', out_shape=[shape] * ARRAYS,...  75 us
    pallas_call x1, Pallas kernels, settle(): pl.pallas_call(settle_kernel, name='settle_results', out_shape=[jax.Shape...  2.2 us

profile of v5, /device:TPU:1, one launch (start us, length us, event | category | flops | bytes accessed | tf_op | source)
XLA Modules:
  0.0 77.9 jit_solution(922155430532441339)
XLA Ops:
  0.6 75.0 %attend_windows.1 = (bf16[64,3072]{1,0:T(8,128)(2,1)}, bf16[64,3072]{1,0:T(8,128)(2,1)}, bf16[64,3072]{1,0:T(8,128)(2,1)}, bf16[64,3072]{1,0:T(8,128)(2,1)}) custom-call(s32[256]{0:T(256)} %slot_stretch_whole.1, s32[256]{0:T(256)} %doc_id_whole.1, s32[256]{0:T(256)} %diag_kind_whole.1, bf16[2,128,768]{2,1,0:T(8,128)(2,1)} %bitcast.4, ...), custom_call_target="tpu_custom_call" | custom-call | tf_op jit(solution)/shard_map/attend_windows/pallas_call | solution.py:443
  75.7 2.2 %settle_results.1 = (bf16[64,3072]{1,0:T(8,128)(2,1)}, bf16[64,3072]{1,0:T(8,128)(2,1)}, bf16[64,3072]{1,0:T(8,128)(2,1)}, bf16[64,3072]{1,0:T(8,128)(2,1)}) custom-call(bf16[64,3072]{1,0:T(8,128)(2,1)} %get-tuple-element.8.refs_0_, bf16[64,3072]{1,0:T(8,128)(2,1)} %get-tuple-element.9.refs_1_, bf16[64,3072]{1,0:T(8,128)(2,1)} %get-tuple-element.10.refs_2_, ...), custom_call_target="tpu_custom_call" | custom-call | tf_op jit(solution)/shard_map/settle_results/pallas_call | solution.py:417

commit v6 on v5

--- a/solution.py
+++ b/solution.py
@@ -252,7 +252,8 @@
 
     def send(array):
         def one(step, carry):
-            peer_member = member ^ (GROUP // 2 ^ step // HP)
+            turn = step // HP
+            peer_member = member ^ (jnp.where(turn < GROUP // 2, 4, 6) ^ turn)
             peer_hp = lax.rem(step, HP)
             peer = peer_member * HP + peer_hp
 

time: 79.4 us -> 79.4 us (level)
  no operation moved by 1% of the time
where the time goes in v6:
time: 79.4 us; the launch traced here: 77.9 us
  Pallas kernels  77.2 us (97%)
    pallas_call x1, Pallas kernels, body(): pl.pallas_call(kernel, name='attend_windows', out_shape=[shape] * ARRAYS,...  75 us
    pallas_call x1, Pallas kernels, settle(): pl.pallas_call(settle_kernel, name='settle_results', out_shape=[jax.Shape...  2.2 us

profile of v6, /device:TPU:1, one launch (start us, length us, event | category | flops | bytes accessed | tf_op | source)
XLA Modules:
  0.0 77.9 jit_solution(9341812875514803816)
XLA Ops:
  0.6 75.0 %attend_windows.1 = (bf16[64,3072]{1,0:T(8,128)(2,1)}, bf16[64,3072]{1,0:T(8,128)(2,1)}, bf16[64,3072]{1,0:T(8,128)(2,1)}, bf16[64,3072]{1,0:T(8,128)(2,1)}) custom-call(s32[256]{0:T(256)} %slot_stretch_whole.1, s32[256]{0:T(256)} %doc_id_whole.1, s32[256]{0:T(256)} %diag_kind_whole.1, bf16[2,128,768]{2,1,0:T(8,128)(2,1)} %bitcast.4, ...), custom_call_target="tpu_custom_call" | custom-call | tf_op jit(solution)/shard_map/attend_windows/pallas_call | solution.py:444
  75.7 2.2 %settle_results.1 = (bf16[64,3072]{1,0:T(8,128)(2,1)}, bf16[64,3072]{1,0:T(8,128)(2,1)}, bf16[64,3072]{1,0:T(8,128)(2,1)}, bf16[64,3072]{1,0:T(8,128)(2,1)}) custom-call(bf16[64,3072]{1,0:T(8,128)(2,1)} %get-tuple-element.8.refs_0_, bf16[64,3072]{1,0:T(8,128)(2,1)} %get-tuple-element.9.refs_1_, bf16[64,3072]{1,0:T(8,128)(2,1)} %get-tuple-element.10.refs_2_, ...), custom_call_target="tpu_custom_call" | custom-call | tf_op jit(solution)/shard_map/settle_results/pallas_call | solution.py:418
